TPU v7x, 32 devices: a whole 2x2x4 slice. The times are simulated.
32 devices in a mesh: groups: 2 (over x), cache: 16 (over z, y, core).
Axes of the slice: x: 2, y: 2, z: 4, core: 2. Of those that a mesh axis runs over, the one named last changes fastest.
Arguments:
- page_store: bfloat16 [8192, 8, 1024], P(('groups', 'cache')), parts along dimension 0, may hold values from -6 to 6
- page_table: int32 [32, 256], P(('groups', 'cache')), parts along dimension 0, may hold values from 0 to 255, each once within a row
- recomp_pos: int32 [32, 128], P(('groups', 'cache')), parts along dimension 0, may hold values from 0 to 2047, as said below
- queries: bfloat16 [32, 128, 4096], P(('groups', 'cache')), parts along dimension 0, may hold values from -135 to 135
- fresh_kv: bfloat16 [32, 128, 1024], P(('groups', 'cache')), parts along dimension 0, may hold values from -5 to 5
Outputs:
- new_store: bfloat16 [8192, 8, 1024], P(('groups', 'cache')), parts along dimension 0
- attended: bfloat16 [32, 128, 4096], P(('groups', 'cache')), parts along dimension 0
There are 2 independent parts, one for each index of `groups`. A program takes and returns all parts, laid end to end along the dimension named above; each array names one. Nothing has to cross between parts.
Inputs may be any that keep to these rules, and one draw needn't show every extreme that they name: `recomp_pos`: for each request the positions rise strictly, no two lie in one page of 8 tokens, and all lie in the first c * 512 tokens, where c, from 2 to 4, is the request's number of spans; some request joins 4 spans.
All inputs are finite; a program needn't handle non-finite values.
Results may differ from a plain program's by a relative error of at most 0.0039.
Values may be sent and summed in bfloat16 or wider, within the bound.
A program may use at most 64 MiB of HBM per device.

v0:
```python
import math

import jax
import jax.numpy as jnp
from jax import lax
from jax.sharding import PartitionSpec as P

HQ = 32
KVH = 4
HD = 128


def attend(query_rows, ordered, positions, block_count, block_rows):
    row_count = query_rows.shape[0]
    group_size = HQ // KVH
    key_width = KVH * HD
    score_scale = 1.0 / math.sqrt(HD)
    q_heads = query_rows.reshape(row_count, KVH, group_size, HD).transpose(1, 2, 0, 3)
    q_heads = q_heads.reshape(KVH, group_size * row_count, HD)
    query_pos = jnp.tile(positions, group_size)

    def advance(block_index, carried):
        run_max, run_sum, accumulated = carried
        first_row = block_index * block_rows
        block_kv = lax.dynamic_slice_in_dim(ordered, first_row, block_rows, 0)
        key_rows = block_kv[:, :key_width].reshape(block_rows, KVH, HD)
        value_rows = block_kv[:, key_width:].reshape(block_rows, KVH, HD)
        scores = (
            jnp.einsum("gqd,kgd->gqk", q_heads, key_rows, preferred_element_type=jnp.float32)
            * score_scale
        )
        key_pos = first_row + jnp.arange(block_rows, dtype=jnp.int32)
        scores = jnp.where(key_pos[None, None, :] <= query_pos[None, :, None], scores, -1e30)
        new_max = jnp.maximum(run_max, jnp.max(scores, axis=-1))
        shrink = jnp.exp(run_max - new_max)
        weights = jnp.exp(scores - new_max[..., None])
        run_sum = run_sum * shrink + jnp.sum(weights, axis=-1)
        product = jnp.einsum(
            "gqk,kgd->gqd",
            weights.astype(jnp.bfloat16),
            value_rows,
            preferred_element_type=jnp.float32,
        )
        accumulated = accumulated * shrink[..., None] + product
        return (new_max, run_sum, accumulated)

    initial = (
        jnp.full((KVH, group_size * row_count), -1e30, jnp.float32),
        jnp.zeros((KVH, group_size * row_count), jnp.float32),
        jnp.zeros((KVH, group_size * row_count, HD), jnp.float32),
    )
    run_max, run_sum, accumulated = lax.fori_loop(0, block_count, advance, initial)
    mixed = (
        (accumulated / run_sum[..., None])
        .reshape(KVH, group_size, row_count, HD)
        .transpose(2, 0, 1, 3)
    )
    return mixed.reshape(row_count, HQ * HD).astype(jnp.bfloat16)


def body(page_store, page_table, recomp_pos, queries, fresh_kv):
    peer_count = lax.axis_size("cache")
    page_count, page_len, row_width = page_store.shape
    per_peer = page_count // peer_count
    page_order = page_table[0]
    positions = recomp_pos[0]
    arrived = lax.all_to_all(
        page_store.reshape(peer_count, per_peer, page_len, row_width),
        "cache",
        split_axis=0,
        concat_axis=0,
        tiled=True,
    )
    received = arrived.reshape(page_count, page_len, row_width)
    ordered = (
        received[page_order]
        .reshape(page_count * page_len, row_width)
        .at[positions]
        .set(fresh_kv[0])
    )
    updated = received.at[page_order].set(ordered.reshape(page_count, page_len, row_width))
    returned = lax.all_to_all(
        updated.reshape(peer_count, per_peer, page_len, row_width),
        "cache",
        split_axis=0,
        concat_axis=0,
        tiled=True,
    )
    new_store = returned.reshape(page_count, page_len, row_width)
    total_keys = page_count * page_len
    block_rows = min(512, total_keys)
    block_count = total_keys // block_rows
    attended = attend(queries[0], ordered, positions, block_count, block_rows)
    return (new_store, attended[None])


def solution(mesh):
    return jax.shard_map(
        body,
        mesh=mesh,
        in_specs=(
            P(("groups", "cache"), None, None),
            P(("groups", "cache"), None),
            P(("groups", "cache"), None),
            P(("groups", "cache"), None, None),
            P(("groups", "cache"), None, None),
        ),
        out_specs=(P(("groups", "cache"), None, None), P(("groups", "cache"), None, None)),
        check_vma=False,
    )
```

profile of v0, /device:TPU:9, one launch (start us, length us, event | category | flops | bytes accessed | tf_op | source)
XLA Modules:
  0.0 244.5 jit_solution(13119390806784643712)
XLA Ops:
  0.6 0.0 copy-start
  0.6 0.0 copy-start.3
  0.7 6.8 %all-to-all-start = ((bf16[16,16,8,1024]{3,2,1,0:T(8,128)(2,1)}), bf16[16,16,8,1024]{3,2,1,0:T(8,128)(2,1)}, u32[]{:S(2)}, u32[]{:S(2)}) async-start(bf16[16,16,8,1024]{3,2,1,0:T(8,128)(2,1)} %bitcast.74), calls=%async_computation | async-start | bytes 8388608 | tf_op jit(solution)/shard_map/all_to_all | solution.py:67
  7.4 0.0 copy-start.4
  7.5 0.0 copy-done.3
  7.5 0.2 copy.28
  7.7 0.4 copy.19
  8.1 0.0 copy-done.5
  8.2 0.0 copy-done.4
  8.2 89.5 %all-to-all-done = bf16[16,16,8,1024]{3,2,1,0:T(8,128)(2,1)} async-done(((bf16[16,16,8,1024]{3,2,1,0:T(8,128)(2,1)}), bf16[16,16,8,1024]{3,2,1,0:T(8,128)(2,1)}, u32[]{:S(2)}, u32[]{:S(2)}) %all-to-all-start) | async-done | bytes 4194336 | tf_op jit(solution)/shard_map/all_to_all | solution.py:67
  97.7 5.0 %gather_fusion = bf16[256,8,1024]{2,1,0:T(8,128)(2,1)} fusion(bf16[256,8,1024]{2,1,0:T(8,128)(2,1)} %bitcast.1, s32[1024]{0:T(1024)S(1)} %pad_clamp_fusion), kind=kCustom, calls=%fused_computation | custom fusion | bytes 8389632 | tf_op jit(solution)/shard_map/gather | solution.py:76
  102.7 0.0 copy-done
  102.7 6.1 %scatter_custom_fusion = bf16[2048,1024]{1,0:T(8,128)(2,1)} fusion(bf16[2048,1024]{1,0:T(8,128)(2,1)} %bitcast.69, s32[128]{0:T(128)S(1)} %fusion.19, bf16[1,128,1024]{2,1,0:T(8,128)(2,1)S(1)} %copy-done), kind=kCustom, calls=%fused_computation.28 | custom fusion | bytes 4456448 | tf_op jit(solution)/shard_map/scatter | solution.py:79
  108.9 33.6 %scatter_fusion = bf16[256,8,1024]{2,1,0:T(8,128)(2,1)} fusion(bf16[256,8,1024]{2,1,0:T(8,128)(2,1)} %bitcast.1, s32[256]{0:T(256)S(1)} %bitcast.80, bf16[256,8,1024]{2,1,0:T(8,128)(2,1)} %bitcast.70), kind=kCustom, calls=%fused_computation.2 | custom fusion | bytes 12583936 | tf_op jit(solution)/shard_map/scatter | solution.py:81
  142.5 7.0 %all-to-all-start.1 = ((bf16[16,16,8,1024]{3,2,1,0:T(8,128)(2,1)}), bf16[16,16,8,1024]{3,2,1,0:T(8,128)(2,1)}, u32[]{:S(2)}, u32[]{:S(2)}) async-start(bf16[16,16,8,1024]{3,2,1,0:T(8,128)(2,1)} %bitcast.9), calls=%async_computation.1 | async-start | bytes 8388608 | tf_op jit(solution)/shard_map/all_to_all | solution.py:82
  149.5 42.9 %while.18 = (s32[]{:T(128)}, f32[4,1024]{1,0:T(4,128)S(1)}, f32[4,1024]{1,0:T(4,128)S(1)}, f32[4,1024,128]{2,1,0:T(8,128)}, bf16[2048,1024]{1,0:T(8,128)(2,1)}, ...) while((s32[]{:T(128)}, f32[4,1024]{1,0:T(4,128)S(1)}, ...), condition=%wide.region_5.6_spmd.clone, body=%wide.region_2.5_spmd.clone.sunk | while | flops 1098928640 | bytes 54801156 | solution.py:52
  149.6 0.4 broadcast_compare_fusion.2
  150.0 1.3 fusion.37
  151.2 0.2 copy.33
  151.5 0.2 copy.34
  151.7 1.8 fusion.38
  153.5 0.0 copy-start.1
  153.5 1.9 fusion.39
  155.4 0.0 copy-done.1
  155.4 3.5 %fusion.41 = f32[4,1024,128]{2,1,0:T(8,128)S(1)} fusion(f32[4,1024,128]{2,1,0:T(8,128)S(1)} %copy-done.1, bf16[512,4,128]{0,2,1:T(8,128)(2,1)S(1)} %bitcast.72, f32[4,512,1024]{2,1,0:T(8,128)S(1)} %get-tuple-element.234, f32[4,1024]{1,0:T(4,128)S(1)} %select_maximum_fusion.2, pred[1024,512]{0,1:T(8,128)(4,1)S(1)} %broadcast_compare_fusion.2, ...), kind=kOutput, calls=%fused_computation.15.clone.1 | convolution fusion | flops 546832384 | bytes 13664257 | tf_op jit(solution)/shard_map/while/body/eval_jaxpr/gqk,kgd->gqd/dot_general | solution.py:38
  159.0 0.0 copy-start.2
  159.0 1.3 copy-done.2
  160.3 0.4 broadcast_compare_fusion.2
  160.7 1.3 fusion.37
  162.0 0.2 copy.33
  162.2 0.2 copy.34
  162.4 1.8 fusion.38
  164.2 0.0 copy-start.1
  164.2 1.9 fusion.39
  166.1 0.0 copy-done.1
  166.1 3.5 %fusion.41 = f32[4,1024,128]{2,1,0:T(8,128)S(1)} fusion(f32[4,1024,128]{2,1,0:T(8,128)S(1)} %copy-done.1, bf16[512,4,128]{0,2,1:T(8,128)(2,1)S(1)} %bitcast.72, f32[4,512,1024]{2,1,0:T(8,128)S(1)} %get-tuple-element.234, f32[4,1024]{1,0:T(4,128)S(1)} %select_maximum_fusion.2, pred[1024,512]{0,1:T(8,128)(4,1)S(1)} %broadcast_compare_fusion.2, ...), kind=kOutput, calls=%fused_computation.15.clone.1 | convolution fusion | flops 546832384 | bytes 13664257 | tf_op jit(solution)/shard_map/while/body/eval_jaxpr/gqk,kgd->gqd/dot_general | solution.py:38
  169.7 0.0 copy-start.2
  169.7 1.3 copy-done.2
  171.0 0.4 broadcast_compare_fusion.2
  171.4 1.3 fusion.37
  172.7 0.2 copy.33
  172.9 0.2 copy.34
  173.1 1.8 fusion.38
  174.9 0.0 copy-start.1
  174.9 1.9 fusion.39
  176.8 0.0 copy-done.1
  176.8 3.5 %fusion.41 = f32[4,1024,128]{2,1,0:T(8,128)S(1)} fusion(f32[4,1024,128]{2,1,0:T(8,128)S(1)} %copy-done.1, bf16[512,4,128]{0,2,1:T(8,128)(2,1)S(1)} %bitcast.72, f32[4,512,1024]{2,1,0:T(8,128)S(1)} %get-tuple-element.234, f32[4,1024]{1,0:T(4,128)S(1)} %select_maximum_fusion.2, pred[1024,512]{0,1:T(8,128)(4,1)S(1)} %broadcast_compare_fusion.2, ...), kind=kOutput, calls=%fused_computation.15.clone.1 | convolution fusion | flops 546832384 | bytes 13664257 | tf_op jit(solution)/shard_map/while/body/eval_jaxpr/gqk,kgd->gqd/dot_general | solution.py:38
  180.4 0.0 copy-start.2
  180.4 1.3 copy-done.2
  181.7 0.4 broadcast_compare_fusion.2
  182.1 1.3 fusion.37
  183.4 0.2 copy.33
  183.6 0.2 copy.34
  183.8 1.8 fusion.38
  185.6 0.0 copy-start.1
  185.7 1.9 fusion.39
  187.6 3.5 %fusion.41 = f32[4,1024,128]{2,1,0:T(8,128)S(1)} fusion(f32[4,1024,128]{2,1,0:T(8,128)S(1)} %copy-done.1, bf16[512,4,128]{0,2,1:T(8,128)(2,1)S(1)} %bitcast.72, f32[4,512,1024]{2,1,0:T(8,128)S(1)} %get-tuple-element.234, f32[4,1024]{1,0:T(4,128)S(1)} %select_maximum_fusion.2, pred[1024,512]{0,1:T(8,128)(4,1)S(1)} %broadcast_compare_fusion.2, ...), kind=kOutput, calls=%fused_computation.15.clone.1 | convolution fusion | flops 546832384 | bytes 13664257 | tf_op jit(solution)/shard_map/while/body/eval_jaxpr/gqk,kgd->gqd/dot_general | solution.py:38
  191.1 0.0 copy-start.2
  191.1 1.3 copy-done.2
  192.5 2.0 divide_convert_fusion
  194.4 0.7 copy.30
  195.1 1.3 convert_element_type.29
  196.4 43.5 %all-to-all-done.1 = bf16[16,16,8,1024]{3,2,1,0:T(8,128)(2,1)} async-done(((bf16[16,16,8,1024]{3,2,1,0:T(8,128)(2,1)}), bf16[16,16,8,1024]{3,2,1,0:T(8,128)(2,1)}, u32[]{:S(2)}, u32[]{:S(2)}) %all-to-all-start.1) | async-done | bytes 4194336 | tf_op jit(solution)/shard_map/all_to_all | solution.py:82
  239.9 4.6 %copy.50 = bf16[256,8,1024]{2,1,0:T(8,128)(2,1)} copy(bf16[256,8,1024]{2,1,0:T(8,128)(2,1)} %bitcast.10) | data formatting | bytes 8388608
  (28 shorter events, 0.2 us)
Async XLA Ops:
  0.6 102.1 %copy-start = (bf16[1,128,1024]{2,1,0:T(8,128)(2,1)S(1)}, bf16[1,128,1024]{2,1,0:T(8,128)(2,1)}, u32[]{:S(2)}) copy-start(bf16[1,128,1024]{2,1,0:T(8,128)(2,1)} %param.11) | copy-start | bytes 786436
  0.6 6.8 %copy-start.3 = (bf16[1,128,4096]{2,1,0:T(8,128)(2,1)S(1)}, bf16[1,128,4096]{2,1,0:T(8,128)(2,1)}, u32[]{:S(2)}) copy-start(bf16[1,128,4096]{2,1,0:T(8,128)(2,1)} %param.10) | copy-start | bytes 3145732
  0.7 97.1 %all-to-all-start = ((bf16[16,16,8,1024]{3,2,1,0:T(8,128)(2,1)}), bf16[16,16,8,1024]{3,2,1,0:T(8,128)(2,1)}, u32[]{:S(2)}, u32[]{:S(2)}) async-start(bf16[16,16,8,1024]{3,2,1,0:T(8,128)(2,1)} %bitcast.74), calls=%async_computation | async-start | bytes 8388608 | tf_op jit(solution)/shard_map/all_to_all | solution.py:67
  7.4 0.7 copy-start.5
  7.4 0.8 copy-start.4
  142.5 97.3 %all-to-all-start.1 = ((bf16[16,16,8,1024]{3,2,1,0:T(8,128)(2,1)}), bf16[16,16,8,1024]{3,2,1,0:T(8,128)(2,1)}, u32[]{:S(2)}, u32[]{:S(2)}) async-start(bf16[16,16,8,1024]{3,2,1,0:T(8,128)(2,1)} %bitcast.9), calls=%async_computation.1 | async-start | bytes 8388608 | tf_op jit(solution)/shard_map/all_to_all | solution.py:82
  153.5 1.9 copy-start.1
  159.0 1.4 copy-start.2
  164.2 1.9 copy-start.1
  169.7 1.4 copy-start.2
  174.9 1.9 copy-start.1
  180.4 1.4 copy-start.2
  185.6 1.9 copy-start.1
  191.1 1.4 copy-start.2
where the time goes:
time: 247 us; the launch traced here: 245 us
  waiting for transfers between devices  133 us (54%)
  local copies, waits for them, and re-layouts  64.2 us (26%)
  matrix products  21.4 us (9%)
  starting transfers between devices  13.8 us (6%)
  other arithmetic  11 us (4%)
    all_to_all x1, waiting for transfers between devices, body(): lax.all_to_all(page_store.reshape(peer_count, per_peer, page_len, row_wid...  89.5 us
    all_to_all x1, waiting for transfers between devices, body(): lax.all_to_all(updated.reshape(peer_count, per_peer, page_len, row_width)...  43.5 us
    scatter x1, local copies, waits for them, and re-layouts, body(): received.at[page_order]  33.6 us
    dot_general x4, matrix products, advance(): jnp.einsum('gqk,kgd->gqd', weights.astype(jnp.bfloat16), value_rows, pref...  14.2 us
    reduce_sum x4, other arithmetic, advance(): run_sum = run_sum * shrink + jnp.sum(weights, axis=-1)  7.43 us
    dot_general x4, matrix products, advance(): jnp.einsum('gqd,kgd->gqk', q_heads, key_rows, preferred_element_type=jnp....  7.18 us
    while x28, local copies, waits for them, and re-layouts  7.06 us
    all_to_all x1, starting transfers between devices, body(): lax.all_to_all(updated.reshape(peer_count, per_peer, page_len, row_width)...  7.03 us
  transfers between devices with their start and end apart: 2, of which 2 were waited for; matrix products, arithmetic and copies ran while one was open for 17% of the time, Pallas kernels for 0%

commit v1 on v0

v1 whole, which is shorter than its diff:
```python
import functools
import math

import jax
import jax.numpy as jnp
from jax import lax
from jax.experimental import pallas as pl
from jax.experimental.pallas import tpu as pltpu
from jax.sharding import PartitionSpec as P

HQ = 32
KVH = 4
HD = 128
GROUP = HQ // KVH
CHUNKS = 8
LANES = 128
MESH = pl.DeviceIdType.MESH
NEG = -1e30


def flip(index, bits):
    result = index
    weight = 1
    while weight <= bits:
        if bits & weight:
            own = lax.rem(lax.div(index, weight), 2)
            result = result + weight * (1 - 2 * own)
        weight *= 2
    return result


def chunk_order():
    half = CHUNKS // 2
    order = []
    for k in range(half):
        order += [k, half + k]
    return order


def kernel(
    n,
    table_col,
    pos_row,
    pos_col,
    store_hbm,
    queries_hbm,
    fresh_hbm,
    out_ref,
    rows_ref,
    kv,
    q_in,
    fresh,
    q_heads,
    key_pos,
    bias,
    row_max,
    row_sum,
    acc,
    payload,
    send_sem,
    recv_sem,
    pay_send_sem,
    pay_recv_sem,
    local_sem,
):
    me = lax.axis_index("cache")
    group = lax.axis_index("groups")
    tokens, width = kv.shape
    pages = table_col.shape[0]
    page_len = tokens // pages
    per_peer = pages // n
    piece = tokens // n
    chunk = tokens // CHUNKS
    peers_per_chunk = n // CHUNKS
    recomp = pos_row.shape[1]
    q_rows = GROUP * recomp
    scale = math.log2(math.e) / math.sqrt(HD)

    barrier = pltpu.get_barrier_semaphore()
    for d in range(1, n):
        pl.semaphore_signal(
            barrier, inc=1, device_id=(group, flip(me, d)), device_id_type=MESH
        )
    q_copy = pltpu.make_async_copy(queries_hbm, q_in, local_sem.at[0])
    fresh_copy = pltpu.make_async_copy(fresh_hbm, fresh, local_sem.at[1])
    own_rows = pl.ds(pl.multiple_of(me * piece, piece), piece)
    own_copy = pltpu.make_async_copy(store_hbm.at[own_rows], kv.at[own_rows], local_sem.at[2])
    fresh_copy.start()
    q_copy.start()
    own_copy.start()
    pl.semaphore_wait(barrier, n - 1)

    def piece_copy(d):
        peer = flip(me, d)
        return pltpu.make_async_remote_copy(
            src_ref=store_hbm.at[pl.ds(pl.multiple_of(peer * piece, piece), piece)],
            dst_ref=kv.at[own_rows],
            send_sem=send_sem.at[d],
            recv_sem=recv_sem.at[d],
            device_id=(group, peer),
            device_id_type=MESH,
        )

    def pay_copy(d):
        peer = flip(me, d)
        return pltpu.make_async_remote_copy(
            src_ref=payload.at[peer],
            dst_ref=rows_ref.at[me],
            send_sem=pay_send_sem.at[d],
            recv_sem=pay_recv_sem.at[d],
            device_id=(group, peer),
            device_id_type=MESH,
        )

    order = chunk_order()
    for k in order:
        for d in range(k * peers_per_chunk, (k + 1) * peers_per_chunk):
            if d:
                piece_copy(d).start()

    slot_ids = lax.broadcasted_iota(jnp.int32, (pages, recomp), 0)
    page_of = lax.div(pos_row[...], page_len)
    lane_of = lax.rem(pos_row[...], page_len)
    slot_of = jnp.sum(
        jnp.where(slot_ids == page_of, table_col[...], 0), axis=0, keepdims=True
    )
    hit = slot_ids == slot_of
    lane = page_len + jnp.sum(
        jnp.where(hit, lane_of - page_len, 0).astype(jnp.float32), axis=1, keepdims=True
    )
    fresh_copy.wait()
    by_slot = jnp.dot(
        hit.astype(jnp.bfloat16), fresh[...], preferred_element_type=jnp.float32
    )
    lane = jnp.broadcast_to(lane, (pages, LANES))
    for p in range(n):
        part = slice(p * per_peer, (p + 1) * per_peer)
        payload[p, :, :width] = by_slot[part].astype(jnp.bfloat16)
        payload[p, :, width:] = lane[part].astype(jnp.bfloat16)
    own_pay = pltpu.make_async_copy(payload.at[me], rows_ref.at[me], local_sem.at[3])
    own_pay.start()
    for d in range(1, n):
        pay_copy(d).start()

    def positions(k, carry):
        start = pl.multiple_of(k * chunk, chunk)
        token = start + lax.broadcasted_iota(jnp.int32, (pages, chunk), 1)
        page = lax.broadcasted_iota(jnp.int32, (pages, chunk), 0)
        place = jnp.sum(
            jnp.where(table_col[...] == lax.div(token, page_len), page, 0),
            axis=0,
            keepdims=True,
        )
        place = place * page_len + lax.rem(token[:1], page_len)
        stale = jnp.max(
            jnp.where(place == pos_col[...], 1, 0), axis=0, keepdims=True
        )
        key_pos[:, pl.ds(start, chunk)] = jnp.where(stale > 0, 2**30, place)
        return carry

    lax.fori_loop(0, CHUNKS, positions, 0)

    q_copy.wait()
    for h in range(HQ):
        g, i = h // GROUP, h % GROUP
        q_heads[g, i * recomp : (i + 1) * recomp, :] = q_in[:, h * HD : (h + 1) * HD]

    def scores_of(g, keys, block_bias):
        raw = lax.dot_general(
            q_heads[g], keys, (((1,), (1,)), ((), ())), preferred_element_type=jnp.float32
        )
        cols = keys.shape[0]
        shaped = raw.reshape(GROUP, recomp, cols) * scale + block_bias[None]
        return shaped.reshape(q_rows, cols)

    def lane_sums(weights):
        total = weights[:, :LANES]
        for c in range(LANES, weights.shape[1], LANES):
            total = total + weights[:, c : c + LANES]
        return total

    bias_fresh = jnp.where(pos_row[...] <= pos_col[...], 0.0, NEG)

    for g in range(KVH):
        keys = fresh[:, g * HD : (g + 1) * HD]
        values = fresh[:, (KVH + g) * HD : (KVH + g + 1) * HD]
        s = scores_of(g, keys, bias_fresh)
        m = jnp.max(s, axis=1, keepdims=True)
        w = jnp.exp2(s - m)
        row_max[g] = jnp.broadcast_to(m, (q_rows, LANES))
        row_sum[g] = lane_sums(w)
        acc[g] = jnp.dot(
            w.astype(jnp.bfloat16), values, preferred_element_type=jnp.float32
        )

    for k in order:
        for d in range(k * peers_per_chunk, (k + 1) * peers_per_chunk):
            if d:
                piece_copy(d).wait_recv()
            else:
                own_copy.wait()
        first = flip(lax.div(me, peers_per_chunk), k) * chunk
        rows = pl.ds(pl.multiple_of(first, chunk), chunk)
        bias[...] = jnp.where(key_pos[:, rows] <= pos_col[...], 0.0, NEG)

        def one_group(g, carry):
            keys = kv[rows, pl.ds(pl.multiple_of(g * HD, HD), HD)]
            values = kv[rows, pl.ds(pl.multiple_of((KVH + g) * HD, HD), HD)]
            s = scores_of(g, keys, bias[...])
            old = row_max[g]
            new = jnp.maximum(old, jnp.max(s, axis=1, keepdims=True))
            shrink = jnp.exp2(old - new)
            w = jnp.exp2(s - new[:, :1])
            row_max[g] = new
            row_sum[g] = row_sum[g] * shrink + lane_sums(w)
            acc[g] = acc[g] * shrink + jnp.dot(
                w.astype(jnp.bfloat16), values, preferred_element_type=jnp.float32
            )
            return carry

        lax.fori_loop(0, KVH, one_group, 0)

    for h in range(HQ):
        g, i = h // GROUP, h % GROUP
        part = slice(i * recomp, (i + 1) * recomp)
        total = jnp.sum(row_sum[g, part, :], axis=1, keepdims=True)
        out_ref[:, h * HD : (h + 1) * HD] = (acc[g, part, :] / total).astype(out_ref.dtype)

    own_pay.wait()
    for d in range(1, n):
        piece_copy(d).wait_send()
        pay_copy(d).wait()


def body(n, page_store, page_table, recomp_pos, queries, fresh_kv):
    pages, page_len, width = page_store.shape
    tokens = pages * page_len
    recomp = recomp_pos.shape[1]
    per_peer = pages // n
    q_rows = GROUP * recomp
    vmem = pl.BlockSpec(memory_space=pltpu.VMEM)
    anywhere = pl.BlockSpec(memory_space=pl.ANY)
    attended, rows = pl.pallas_call(
        functools.partial(kernel, n),
        out_shape=(
            jax.ShapeDtypeStruct((recomp, HQ * HD), jnp.bfloat16),
            jax.ShapeDtypeStruct((n, per_peer, width + LANES), jnp.bfloat16),
        ),
        in_specs=[vmem, vmem, vmem, anywhere, anywhere, anywhere],
        out_specs=(vmem, anywhere),
        scratch_shapes=[
            pltpu.VMEM((tokens, width), jnp.bfloat16),
            pltpu.VMEM((recomp, HQ * HD), jnp.bfloat16),
            pltpu.VMEM((recomp, width), jnp.bfloat16),
            pltpu.VMEM((KVH, q_rows, HD), jnp.bfloat16),
            pltpu.VMEM((1, tokens), jnp.int32),
            pltpu.VMEM((recomp, tokens // CHUNKS), jnp.float32),
            pltpu.VMEM((KVH, q_rows, LANES), jnp.float32),
            pltpu.VMEM((KVH, q_rows, LANES), jnp.float32),
            pltpu.VMEM((KVH, q_rows, HD), jnp.float32),
            pltpu.VMEM((n, per_peer, width + LANES), jnp.bfloat16),
            pltpu.SemaphoreType.DMA((n,)),
            pltpu.SemaphoreType.DMA((n,)),
            pltpu.SemaphoreType.DMA((n,)),
            pltpu.SemaphoreType.DMA((n,)),
            pltpu.SemaphoreType.DMA((4,)),
        ],
        compiler_params=pltpu.CompilerParams(
            collective_id=0, has_side_effects=True, vmem_limit_bytes=48 * 2**20
        ),
        name="blend_attend",
    )(
        page_table.reshape(pages, 1),
        recomp_pos,
        recomp_pos.reshape(recomp, 1),
        page_store.reshape(tokens, width),
        queries[0],
        fresh_kv[0],
    )
    paged = page_store.reshape(n, per_peer, page_len, width)
    lane = rows[:, :, width:width + 1].astype(jnp.int32)[:, :, :, None]
    here = lane == jnp.arange(page_len, dtype=jnp.int32)[None, None, :, None]
    new_store = jnp.where(here, rows[:, :, None, :width], paged)
    return (new_store.reshape(pages, page_len, width), attended[None])


def solution(mesh):
    return jax.shard_map(
        functools.partial(body, mesh.shape["cache"]),
        mesh=mesh,
        in_specs=(
            P(("groups", "cache"), None, None),
            P(("groups", "cache"), None),
            P(("groups", "cache"), None),
            P(("groups", "cache"), None, None),
            P(("groups", "cache"), None, None),
        ),
        out_specs=(P(("groups", "cache"), None, None), P(("groups", "cache"), None, None)),
        check_vma=False,
    )
```

time: 247 us -> 120 us (0.49)
  waiting for transfers between devices: 133 us -> 0 us
  Pallas kernels: 0 us -> 109 us
  local copies, waits for them, and re-layouts: 64.2 us -> 5.5 us
  matrix products: 21.4 us -> 0 us
  starting transfers between devices: 13.8 us -> 0 us
  other arithmetic: 11 us -> 4.44 us
    all_to_all x2 -> x0, waiting for transfers between devices: 133 us -> none  [the longest x1 89.5 us: body(): lax.all_to_all(page_store.reshape(peer_count, per_peer, page_len, row_wid...]
    pallas_call x0 -> x1, Pallas kernels: none -> 109 us  [body(): pl.pallas_call(functools.partial(kernel, n), out_shape=(jax.ShapeDtypeStr...]
    scatter x2 -> x0, local copies, waits for them, and re-layouts: 39.8 us -> none  [the longest x1 33.6 us: body(): received.at[page_order]]
    dot_general x8 -> x0, matrix products: 21.4 us -> none  [the longest x4 14.2 us: advance(): jnp.einsum('gqk,kgd->gqd', weights.astype(jnp.bfloat16), value_rows, pref...]
    all_to_all x2 -> x0, starting transfers between devices: 13.8 us -> none  [the longest x1 7.03 us: body(): lax.all_to_all(updated.reshape(peer_count, per_peer, page_len, row_width)...]
    reduce_sum x4 -> x0, other arithmetic: 7.43 us -> none  [advance(): run_sum = run_sum * shrink + jnp.sum(weights, axis=-1)]
    while x28 -> x0, local copies, waits for them, and re-layouts: 7.06 us -> none
    slice x4 -> x1, local copies, waits for them, and re-layouts: 5.11 us -> 0.06 us  [body(): new_store = jnp.where(here, rows[:, :, None, :width], paged)]
  transfers between devices with their start and end apart: 2 -> 0, of which waited for: 2 -> 0; matrix products, arithmetic and copies ran while one was open for 17% -> 0% of each run, Pallas kernels for 0% -> 0%
where the time goes in v1:
time: 120 us; the launch traced here: 119 us
  Pallas kernels  109 us (91%)
  local copies, waits for them, and re-layouts  5.5 us (5%)
  other arithmetic  4.44 us (4%)
    pallas_call x1, Pallas kernels, body(): pl.pallas_call(functools.partial(kernel, n), out_shape=(jax.ShapeDtypeStr...  109 us
    select_n x1, other arithmetic, body(): new_store = jnp.where(here, rows[:, :, None, :width], paged)  3.98 us
    unnamed x7, local copies, waits for them, and re-layouts  3.8 us

profile of v1, /device:TPU:9, one launch (start us, length us, event | category | flops | bytes accessed | tf_op | source)
XLA Modules:
  0.0 119.3 jit_solution(7927112259680978854)
XLA Ops:
  0.6 0.8 copy.9.pos_col
  1.4 0.8 copy.8.table_col
  2.2 0.0 copy-start
  2.2 1.2 %copy-done = bf16[1,128,4096]{2,1,0:T(8,128)(2,1)S(1)} copy-done((bf16[1,128,4096]{2,1,0:T(8,128)(2,1)S(1)}, bf16[1,128,4096]{2,1,0:T(8,128)(2,1)}, u32[]{:S(2)}) %copy-start) | copy-done | bytes 1048600
  3.4 0.0 copy-start.1
  3.4 0.9 copy-done.1
  4.4 0.0 copy-start.2
  4.4 0.7 copy-done.2
  5.0 108.7 %blend_attend.1 = (bf16[128,4096]{1,0:T(8,128)(2,1)S(1)}, bf16[16,16,1152]{2,1,0:T(8,128)(2,1)S(1)}) custom-call(s32[256,1]{1,0:T(8,128)S(1)} %copy.8.table_col, s32[1,128]{1,0:T(1,128)S(1)} %copy-done.2, s32[128,1]{1,0:T(8,128)S(1)} %copy.9.pos_col, bf16[2048,1024]{1,0:T(8,128)(2,1)} %bitcast.11, bf16[128,4096]{1,0:T(8,128)(2,1)S(1)} %bitcast.8, ...), custom_call_target="tpu_custom_call" | custom-call | tf_op jit(solution)/shard_map/blend_attend/pallas_call | solution.py:243
  113.7 0.3 convert_reduce_fusion
  114.1 0.1 slice.7
  114.1 0.1 reshape.34
  114.2 0.1 iota_compare_fusion
  114.3 4.0 %broadcast_select_fusion = bf16[256,8,1024]{2,1,0:T(8,128)(2,1)} fusion(bf16[256,8,1024]{2,1,0:T(8,128)(2,1)} %param.5, pred[256,8]{1,0:T(8,128)(4,1)S(1)} %iota_compare_fusion, bf16[256,1024]{1,0:T(8,128)(2,1)S(1)} %bitcast.12), kind=kLoop, calls=%fused_computation | loop fusion | flops 2097152 | bytes 8914944 | tf_op jit(solution)/shard_map/jit(_where)/select_n | solution.py:283
  118.3 1.0 copy.11
Async XLA Ops:
  2.2 1.2 %copy-start = (bf16[1,128,4096]{2,1,0:T(8,128)(2,1)S(1)}, bf16[1,128,4096]{2,1,0:T(8,128)(2,1)}, u32[]{:S(2)}) copy-start(bf16[1,128,4096]{2,1,0:T(8,128)(2,1)} %param.8) | copy-start | bytes 3145732
  3.4 0.9 copy-start.1
  4.4 0.7 copy-start.2

commit v2 on v1

--- a/solution.py
+++ b/solution.py
@@ -29,6 +29,13 @@
     return result
 
 
+def column(row):
+    size = row.shape[1]
+    down = lax.broadcasted_iota(jnp.int32, (size, size), 0)
+    along = lax.broadcasted_iota(jnp.int32, (size, size), 1)
+    return jnp.sum(jnp.where(down == along, row, 0), axis=1, keepdims=True)
+
+
 def chunk_order():
     half = CHUNKS // 2
     order = []
@@ -39,14 +46,16 @@
 
 def kernel(
     n,
-    table_col,
-    pos_row,
-    pos_col,
+    table_hbm,
+    pos_hbm,
     store_hbm,
     queries_hbm,
     fresh_hbm,
     out_ref,
     rows_ref,
+    lanes_ref,
+    table_row,
+    pos_row,
     kv,
     q_in,
     fresh,
@@ -57,16 +66,19 @@
     row_sum,
     acc,
     payload,
+    lanes,
     send_sem,
     recv_sem,
     pay_send_sem,
     pay_recv_sem,
+    lane_send_sem,
+    lane_recv_sem,
     local_sem,
 ):
     me = lax.axis_index("cache")
     group = lax.axis_index("groups")
     tokens, width = kv.shape
-    pages = table_col.shape[0]
+    pages = table_row.shape[1]
     page_len = tokens // pages
     per_peer = pages // n
     piece = tokens // n
@@ -85,6 +97,10 @@
     fresh_copy = pltpu.make_async_copy(fresh_hbm, fresh, local_sem.at[1])
     own_rows = pl.ds(pl.multiple_of(me * piece, piece), piece)
     own_copy = pltpu.make_async_copy(store_hbm.at[own_rows], kv.at[own_rows], local_sem.at[2])
+    table_copy = pltpu.make_async_copy(table_hbm, table_row, local_sem.at[4])
+    pos_copy = pltpu.make_async_copy(pos_hbm, pos_row, local_sem.at[5])
+    table_copy.start()
+    pos_copy.start()
     fresh_copy.start()
     q_copy.start()
     own_copy.start()
@@ -112,31 +128,49 @@
             device_id_type=MESH,
         )
 
+    def lane_copy(d):
+        return pltpu.make_async_remote_copy(
+            src_ref=lanes,
+            dst_ref=lanes_ref.at[me],
+            send_sem=lane_send_sem.at[d],
+            recv_sem=lane_recv_sem.at[d],
+            device_id=(group, flip(me, d)),
+            device_id_type=MESH,
+        )
+
     order = chunk_order()
     for k in order:
         for d in range(k * peers_per_chunk, (k + 1) * peers_per_chunk):
             if d:
                 piece_copy(d).start()
 
+    table_copy.wait()
+    pos_copy.wait()
+    table_col = column(table_row[...])
+    pos_col = column(pos_row[...])
+
     slot_ids = lax.broadcasted_iota(jnp.int32, (pages, recomp), 0)
     page_of = lax.div(pos_row[...], page_len)
-    lane_of = lax.rem(pos_row[...], page_len)
     slot_of = jnp.sum(
-        jnp.where(slot_ids == page_of, table_col[...], 0), axis=0, keepdims=True
+        jnp.where(slot_ids == page_of, table_col, 0), axis=0, keepdims=True
     )
     hit = slot_ids == slot_of
-    lane = page_len + jnp.sum(
-        jnp.where(hit, lane_of - page_len, 0).astype(jnp.float32), axis=1, keepdims=True
-    )
+    slots = lax.broadcasted_iota(jnp.int32, (recomp, pages), 1)
+    replaced = jnp.where(
+        slots == column(slot_of), lax.rem(pos_col, page_len) - page_len, 0
+    )
+    lanes[...] = page_len + jnp.sum(replaced, axis=0, keepdims=True)
+    own_lanes = pltpu.make_async_copy(lanes, lanes_ref.at[me], local_sem.at[6])
+    own_lanes.start()
+    for d in range(1, n):
+        lane_copy(d).start()
     fresh_copy.wait()
     by_slot = jnp.dot(
         hit.astype(jnp.bfloat16), fresh[...], preferred_element_type=jnp.float32
     )
-    lane = jnp.broadcast_to(lane, (pages, LANES))
     for p in range(n):
         part = slice(p * per_peer, (p + 1) * per_peer)
-        payload[p, :, :width] = by_slot[part].astype(jnp.bfloat16)
-        payload[p, :, width:] = lane[part].astype(jnp.bfloat16)
+        payload[p] = by_slot[part].astype(jnp.bfloat16)
     own_pay = pltpu.make_async_copy(payload.at[me], rows_ref.at[me], local_sem.at[3])
     own_pay.start()
     for d in range(1, n):
@@ -147,13 +181,13 @@
         token = start + lax.broadcasted_iota(jnp.int32, (pages, chunk), 1)
         page = lax.broadcasted_iota(jnp.int32, (pages, chunk), 0)
         place = jnp.sum(
-            jnp.where(table_col[...] == lax.div(token, page_len), page, 0),
+            jnp.where(table_col == lax.div(token, page_len), page, 0),
             axis=0,
             keepdims=True,
         )
         place = place * page_len + lax.rem(token[:1], page_len)
         stale = jnp.max(
-            jnp.where(place == pos_col[...], 1, 0), axis=0, keepdims=True
+            jnp.where(place == pos_col, 1, 0), axis=0, keepdims=True
         )
         key_pos[:, pl.ds(start, chunk)] = jnp.where(stale > 0, 2**30, place)
         return carry
@@ -179,7 +213,7 @@
             total = total + weights[:, c : c + LANES]
         return total
 
-    bias_fresh = jnp.where(pos_row[...] <= pos_col[...], 0.0, NEG)
+    bias_fresh = jnp.where(pos_row[...] <= pos_col, 0.0, NEG)
 
     for g in range(KVH):
         keys = fresh[:, g * HD : (g + 1) * HD]
@@ -201,7 +235,7 @@
                 own_copy.wait()
         first = flip(lax.div(me, peers_per_chunk), k) * chunk
         rows = pl.ds(pl.multiple_of(first, chunk), chunk)
-        bias[...] = jnp.where(key_pos[:, rows] <= pos_col[...], 0.0, NEG)
+        bias[...] = jnp.where(key_pos[:, rows] <= pos_col, 0.0, NEG)
 
         def one_group(g, carry):
             keys = kv[rows, pl.ds(pl.multiple_of(g * HD, HD), HD)]
@@ -226,9 +260,11 @@
         total = jnp.sum(row_sum[g, part, :], axis=1, keepdims=True)
         out_ref[:, h * HD : (h + 1) * HD] = (acc[g, part, :] / total).astype(out_ref.dtype)
 
+    own_lanes.wait()
     own_pay.wait()
     for d in range(1, n):
         piece_copy(d).wait_send()
+        lane_copy(d).wait()
         pay_copy(d).wait()
 
 
@@ -239,16 +275,19 @@
     per_peer = pages // n
     q_rows = GROUP * recomp
     vmem = pl.BlockSpec(memory_space=pltpu.VMEM)
-    anywhere = pl.BlockSpec(memory_space=pl.ANY)
-    attended, rows = pl.pallas_call(
+    hbm = pl.BlockSpec(memory_space=pltpu.HBM)
+    attended, rows, lanes = pl.pallas_call(
         functools.partial(kernel, n),
         out_shape=(
             jax.ShapeDtypeStruct((recomp, HQ * HD), jnp.bfloat16),
-            jax.ShapeDtypeStruct((n, per_peer, width + LANES), jnp.bfloat16),
+            jax.ShapeDtypeStruct((n, per_peer, width), jnp.bfloat16),
+            jax.ShapeDtypeStruct((n, 1, pages), jnp.int32),
         ),
-        in_specs=[vmem, vmem, vmem, anywhere, anywhere, anywhere],
-        out_specs=(vmem, anywhere),
+        in_specs=[hbm] * 5,
+        out_specs=(vmem, hbm, hbm),
         scratch_shapes=[
+            pltpu.VMEM((1, pages), jnp.int32),
+            pltpu.VMEM((1, recomp), jnp.int32),
             pltpu.VMEM((tokens, width), jnp.bfloat16),
             pltpu.VMEM((recomp, HQ * HD), jnp.bfloat16),
             pltpu.VMEM((recomp, width), jnp.bfloat16),
@@ -258,29 +297,32 @@
             pltpu.VMEM((KVH, q_rows, LANES), jnp.float32),
             pltpu.VMEM((KVH, q_rows, LANES), jnp.float32),
             pltpu.VMEM((KVH, q_rows, HD), jnp.float32),
-            pltpu.VMEM((n, per_peer, width + LANES), jnp.bfloat16),
-            pltpu.SemaphoreType.DMA((n,)),
-            pltpu.SemaphoreType.DMA((n,)),
-            pltpu.SemaphoreType.DMA((n,)),
-            pltpu.SemaphoreType.DMA((n,)),
-            pltpu.SemaphoreType.DMA((4,)),
+            pltpu.VMEM((n, per_peer, width), jnp.bfloat16),
+            pltpu.VMEM((1, pages), jnp.int32),
+            pltpu.SemaphoreType.DMA((n,)),
+            pltpu.SemaphoreType.DMA((n,)),
+            pltpu.SemaphoreType.DMA((n,)),
+            pltpu.SemaphoreType.DMA((n,)),
+            pltpu.SemaphoreType.DMA((n,)),
+            pltpu.SemaphoreType.DMA((n,)),
+            pltpu.SemaphoreType.DMA((7,)),
         ],
         compiler_params=pltpu.CompilerParams(
-            collective_id=0, has_side_effects=True, vmem_limit_bytes=48 * 2**20
+            collective_id=0, has_side_effects=True, vmem_limit_bytes=62 * 2**20
         ),
         name="blend_attend",
     )(
-        page_table.reshape(pages, 1),
+        page_table,
         recomp_pos,
-        recomp_pos.reshape(recomp, 1),
         page_store.reshape(tokens, width),
         queries[0],
         fresh_kv[0],
     )
     paged = page_store.reshape(n, per_peer, page_len, width)
-    lane = rows[:, :, width:width + 1].astype(jnp.int32)[:, :, :, None]
+    first = lax.axis_index("cache") * per_peer
+    lane = lax.dynamic_slice_in_dim(lanes[:, 0], first, per_peer, 1)[:, :, None, None]
     here = lane == jnp.arange(page_len, dtype=jnp.int32)[None, None, :, None]
-    new_store = jnp.where(here, rows[:, :, None, :width], paged)
+    new_store = jnp.where(here, rows[:, :, None, :], paged)
     return (new_store.reshape(pages, page_len, width), attended[None])
 
 

time: 120 us -> 116 us (0.967)
  local copies, waits for them, and re-layouts: 5.5 us -> 1.85 us
    unnamed x7 -> x3, local copies, waits for them, and re-layouts: 3.8 us -> 0.97 us
    reshape x2 -> x0, local copies, waits for them, and re-layouts: 1.57 us -> none  [the longest x1 0.8 us: body(): page_table.reshape(pages, 1)]
where the time goes in v2:
time: 116 us
  Pallas kernels  109 us (94%)
  other arithmetic  4.2 us (4%)
  local copies, waits for them, and re-layouts  1.85 us (2%)
    pallas_call x1, Pallas kernels, body(): pl.pallas_call(functools.partial(kernel, n), out_shape=(jax.ShapeDtypeStr...  109 us
    select_n x1, other arithmetic, body(): new_store = jnp.where(here, rows[:, :, None, :], paged)  4.09 us

profile of v2, /device:TPU:9, one launch (start us, length us, event | category | flops | bytes accessed | tf_op | source)
XLA Modules:
  0.0 115.8 jit_solution(8290599851703751118)
XLA Ops:
  0.6 109.1 %blend_attend.1 = (bf16[128,4096]{1,0:T(8,128)(2,1)}, bf16[16,16,1024]{2,1,0:T(8,128)(2,1)}, s32[16,1,256]{2,1,0:T(1,128)}) custom-call(s32[1,256]{1,0:T(1,128)} %table_hbm.1, s32[1,128]{1,0:T(1,128)} %pos_hbm.1, bf16[2048,1024]{1,0:T(8,128)(2,1)} %bitcast.5, bf16[128,4096]{1,0:T(8,128)(2,1)} %bitcast.6, bf16[128,1024]{1,0:T(8,128)(2,1)} %bitcast.9), custom_call_target="tpu_custom_call" | custom-call | tf_op jit(solution)/shard_map/blend_attend/pallas_call | solution.py:279
  109.7 0.8 dynamic-slice_reduce_fusion
  110.5 0.1 eq.20
  110.6 0.1 iota_compare_fusion
  110.7 0.0 copy-start
  110.7 4.1 %broadcast_select_fusion = bf16[256,8,1024]{2,1,0:T(8,128)(2,1)} fusion(bf16[256,8,1024]{2,1,0:T(8,128)(2,1)} %param.5, pred[256,8]{1,0:T(8,128)(4,1)S(1)} %iota_compare_fusion, bf16[256,1024]{1,0:T(8,128)(2,1)} %bitcast.8), kind=kLoop, calls=%fused_computation | loop fusion | flops 2097152 | bytes 8914944 | tf_op jit(solution)/shard_map/jit(_where)/select_n | solution.py:325
  114.8 0.0 copy-done
  114.8 1.0 copy.8
Async XLA Ops:
  110.7 4.1 %copy-start = (bf16[128,4096]{1,0:T(8,128)(2,1)S(1)}, bf16[128,4096]{1,0:T(8,128)(2,1)}, u32[]{:S(2)}) copy-start(bf16[128,4096]{1,0:T(8,128)(2,1)} %get-tuple-element.7) | copy-start | bytes 3145732

commit v3 on v2

--- a/solution.py
+++ b/solution.py
@@ -37,11 +37,7 @@
 
 
 def chunk_order():
-    half = CHUNKS // 2
-    order = []
-    for k in range(half):
-        order += [k, half + k]
-    return order
+    return list(range(CHUNKS))
 
 
 def kernel(

time: 116 us -> 116 us (level)
  no operation moved by 1% of the time
where the time goes in v3:
time: 116 us
  Pallas kernels  109 us (94%)
  other arithmetic  4.2 us (4%)
  local copies, waits for them, and re-layouts  1.85 us (2%)
    pallas_call x1, Pallas kernels, body(): pl.pallas_call(functools.partial(kernel, n), out_shape=(jax.ShapeDtypeStr...  109 us
    select_n x1, other arithmetic, body(): new_store = jnp.where(here, rows[:, :, None, :], paged)  4.09 us

profile of v3, /device:TPU:9, one launch (start us, length us, event | category | flops | bytes accessed | tf_op | source)
XLA Modules:
  0.0 115.7 jit_solution(16305863235918500119)
XLA Ops:
  0.6 109.0 %blend_attend.1 = (bf16[128,4096]{1,0:T(8,128)(2,1)}, bf16[16,16,1024]{2,1,0:T(8,128)(2,1)}, s32[16,1,256]{2,1,0:T(1,128)}) custom-call(s32[1,256]{1,0:T(1,128)} %table_hbm.1, s32[1,128]{1,0:T(1,128)} %pos_hbm.1, bf16[2048,1024]{1,0:T(8,128)(2,1)} %bitcast.5, bf16[128,4096]{1,0:T(8,128)(2,1)} %bitcast.6, bf16[128,1024]{1,0:T(8,128)(2,1)} %bitcast.9), custom_call_target="tpu_custom_call" | custom-call | tf_op jit(solution)/shard_map/blend_attend/pallas_call | solution.py:275
  109.6 0.8 dynamic-slice_reduce_fusion
  110.4 0.1 eq.20
  110.5 0.1 iota_compare_fusion
  110.6 0.0 copy-start
  110.6 4.1 %broadcast_select_fusion = bf16[256,8,1024]{2,1,0:T(8,128)(2,1)} fusion(bf16[256,8,1024]{2,1,0:T(8,128)(2,1)} %param.5, pred[256,8]{1,0:T(8,128)(4,1)S(1)} %iota_compare_fusion, bf16[256,1024]{1,0:T(8,128)(2,1)} %bitcast.8), kind=kLoop, calls=%fused_computation | loop fusion | flops 2097152 | bytes 8914944 | tf_op jit(solution)/shard_map/jit(_where)/select_n | solution.py:321
  114.7 0.0 copy-done
  114.7 1.0 copy.8
Async XLA Ops:
  110.6 4.1 %copy-start = (bf16[128,4096]{1,0:T(8,128)(2,1)S(1)}, bf16[128,4096]{1,0:T(8,128)(2,1)}, u32[]{:S(2)}) copy-start(bf16[128,4096]{1,0:T(8,128)(2,1)} %get-tuple-element.7) | copy-start | bytes 3145732
